TPU v7x, 256 devices: a whole 4x4x8 slice. The times are simulated.
256 devices in a mesh: row: 32 (over y_hi, z, core), col: 8 (over x, y_lo).
Axes of the slice: x: 4, y: 4 (y_hi: 2, y_lo: 2; y = y_hi * 2 + y_lo), z: 8, core: 2. Of those that a mesh axis runs over, the one named last changes fastest.
Arguments:
- blocks: bfloat16 [320, 288, 128, 128], P('row', 'col')
- slot_cols: int32 [320, 288], P('row', 'col'), may hold values from 0 to 39, as said below
- counts: int32 [320, 8], P('row', 'col'), may hold values from 2 to 36, as said below
- demand: bfloat16 [40960, 128], P('col'), may hold values from 0.1 to 10
- value_added: float32 [40960], P('col'), may hold values from 0.5 to 5
Outputs:
- propagated: bfloat16 [40960, 128], P('row')
Inputs may be any that keep to these rules, and one draw needn't show every extreme that they name: `counts`: some block row has all 36 slots live in every column group; live slots come first in each group. `slot_cols`: within one block row and column group the 36 slots name distinct column blocks.
All inputs are finite; a program needn't handle non-finite values.
Results may differ from a plain program's by a relative error of at most 0.0042.
Values may be sent and summed in bfloat16 or wider, within the bound.
A program may use at most 128 MiB of HBM per device.

v0:
```python
import jax
import jax.numpy as jnp
from jax import lax
from jax.sharding import PartitionSpec as P


def body(blocks, slot_cols, counts, demand, value_added):
    rows_here = blocks.shape[0]
    slot_count = blocks.shape[1]
    block_size = blocks.shape[2]
    demand_width = demand.shape[1]
    group_blocks = demand.shape[0] // block_size
    live_slots = (jnp.arange(slot_count, dtype=jnp.int32)[None, :] < counts).astype(jnp.float32)
    column_sums = jnp.sum(blocks, axis=2, dtype=jnp.float32) * live_slots[:, :, None]
    onehot = (
        slot_cols.reshape(-1)[:, None] == jnp.arange(group_blocks, dtype=jnp.int32)[None, :]
    ).astype(jnp.float32)
    partial_totals = jnp.einsum(
        "nc,nk->ck", onehot, column_sums.reshape(-1, block_size), precision=lax.Precision.HIGHEST
    )
    totals = lax.psum(partial_totals, "row")
    inverse = 1.0 / (totals.reshape(-1) + value_added)
    inverse = inverse.reshape(group_blocks, block_size)
    scaling = inverse[slot_cols] * live_slots[:, :, None]
    coefficients = (blocks * scaling[:, :, None, :]).astype(jnp.bfloat16)

    def local_layer(source):
        picked = source.reshape(group_blocks, block_size, demand_width)[slot_cols]
        product = jnp.einsum(
            "bsij,bsjk->bik", coefficients, picked, preferred_element_type=jnp.float32
        )
        return product.reshape(rows_here * block_size, demand_width)

    group_index = lax.axis_index("col")
    group_rows = group_blocks * block_size
    part_one = local_layer(demand)
    layer_one = lax.psum(part_one, "col").astype(jnp.bfloat16)
    gathered = lax.all_gather(layer_one, "row", axis=0, tiled=True)
    needed = lax.dynamic_slice_in_dim(gathered, group_index * group_rows, group_rows, 0)
    layer_two = lax.psum(local_layer(needed), "col")
    return (layer_one.astype(jnp.float32) + layer_two).astype(jnp.bfloat16)


def solution(mesh):
    return jax.shard_map(
        body,
        mesh=mesh,
        in_specs=(
            P("row", "col", None, None),
            P("row", "col"),
            P("row", "col"),
            P("col", None),
            P("col"),
        ),
        out_specs=P("row", None),
        check_vma=False,
    )
```

profile of v0, /device:TPU:24, one launch (start us, length us, event | category | flops | bytes accessed | tf_op | source)
XLA Modules:
  0.0 430.1 jit_solution(1781961064499498028)
XLA Ops:
  6.5 0.0 copy-start
  6.5 0.0 copy-start.2
  6.5 0.0 all-gather.2.cloned.1.call-start
  6.5 0.9 eq.15
  7.4 0.7 compare_select_fusion
  8.1 0.7 fusion.8
  8.9 0.1 reshape.60
  8.9 0.1 reshape.63
  9.0 8.6 %convert_reduce_fusion = f32[10,36,128]{2,1,0:T(8,128)S(1)} fusion(bf16[10,36,128,128]{3,2,1,0:T(8,128)(2,1)} %param.5), kind=kLoop, calls=%fused_computation.4 | loop fusion | flops 11750400 | bytes 11980800 | tf_op jit(solution)/shard_map/reduce_sum | solution.py:14
  17.7 0.4 convolution_bitcast_fusion
  18.1 134.5 %psum.21 = f32[5120]{0:T(1024)S(1)} all-reduce(f32[5120]{0:T(1024)S(1)} %convolution_bitcast_fusion), channel_id=1, replica_groups=mesh['row'=32,'col'=8] {'row'}, use_global_device_ids=true, to_apply=%region_1.0 | all-reduce | flops 5120 | bytes 40960 | tf_op jit(solution)/shard_map/psum | solution.py:21
  152.6 0.0 copy-done.2
  152.6 1.1 gather_fusion
  153.8 0.1 broadcast_multiply_fusion
  153.9 0.0 copy-done
  153.9 11.1 %gather_fusion.1 = bf16[360,128,128]{2,1,0:T(8,128)(2,1)} fusion(bf16[40,128,128]{2,1,0:T(8,128)(2,1)S(1)} %bitcast.19, s32[1024]{0:T(1024)S(1)} %pad_clamp_fusion), kind=kCustom, calls=%fused_computation.1 | custom fusion | bytes 23594400 | tf_op jit(solution)/shard_map/gather | solution.py:28
  165.0 10.9 %fusion.3 = f32[10,128,128,1]{2,1,3,0:T(8,128)S(1)} fusion(bf16[10,36,128,128]{3,2,1,0:T(8,128)(2,1)} %bitcast.22, bf16[10,36,128,128]{3,2,1,0:T(8,128)(2,1)} %param.5, f32[10,36,128]{2,1,0:T(8,128)S(1)} %broadcast_multiply_fusion), kind=kOutput, calls=%fused_computation.7 | convolution fusion | flops 1527644160 | bytes 24432640 | tf_op jit(solution)/shard_map/bsij,bsjk->bik/dot_general | solution.py:29
  175.9 40.3 %all-reduce.4 = bf16[1280,128]{1,0:T(8,128)(2,1)} all-reduce(f32[1280,128]{1,0:T(8,128)S(1)} %bitcast.24), channel_id=1, replica_groups=mesh['row'=32,'col'=8] {'col'}, use_global_device_ids=true, to_apply=%region_2.0 | all-reduce | flops 163840 | bytes 983040 | tf_op jit(solution)/shard_map/psum | solution.py:37
  216.2 0.0 all-gather.2.cloned.1.call-update
  216.2 0.0 all-reduce.3.cloned.1.call-start
  216.3 103.9 %all-gather.2.cloned.1.call-done = bf16[40960,128]{1,0:T(8,128)(2,1)} async-done(((bf16[1280,128]{1,0:T(8,128)(2,1)}), bf16[40960,128]{1,0:T(8,128)(2,1)}) %all-gather.2.cloned.1.call-update) | async-done | bytes 10485776 | tf_op jit(solution)/shard_map/all_gather | solution.py:38
  320.2 1.4 constant_dynamic-slice_fusion
  321.6 11.1 %gather_fusion.2 = bf16[360,128,128]{2,1,0:T(8,128)(2,1)} fusion(bf16[40,128,128]{2,1,0:T(8,128)(2,1)S(1)} %bitcast.20, s32[1024]{0:T(1024)S(1)} %pad_clamp_fusion), kind=kCustom, calls=%fused_computation.2 | custom fusion | bytes 23594400 | tf_op jit(solution)/shard_map/gather | solution.py:28
  332.7 0.0 copy-start.1
  332.7 11.8 %fusion.1 = f32[10,128,128,1]{2,1,3,0:T(8,128)} fusion(bf16[10,36,128,128]{3,2,1,0:T(8,128)(2,1)} %bitcast.21, bf16[10,36,128,128]{3,2,1,0:T(8,128)(2,1)} %param.5, f32[10,36,128]{2,1,0:T(8,128)S(1)} %broadcast_multiply_fusion), kind=kOutput, calls=%fused_computation.6 | convolution fusion | flops 1527644160 | bytes 24432640 | tf_op jit(solution)/shard_map/bsij,bsjk->bik/dot_general | solution.py:29
  344.5 0.0 all-reduce.3.cloned.1.call-update
  344.5 76.8 %all-reduce.3.cloned.1.call-done = f32[1280,128]{1,0:T(8,128)} async-done(((f32[1280,128]{1,0:T(8,128)}), f32[1280,128]{1,0:T(8,128)}) %all-reduce.3.cloned.1.call-update) | async-done | bytes 655376 | tf_op jit(solution)/shard_map/psum | solution.py:40
  421.4 0.0 copy-done.1
  421.4 1.9 add_convert_fusion
  (4 shorter events, 0.0 us)
Async XLA Ops:
  6.5 147.3 %copy-start = (bf16[5120,128]{1,0:T(8,128)(2,1)S(1)}, bf16[5120,128]{1,0:T(8,128)(2,1)}, u32[]{:S(2)}) copy-start(bf16[5120,128]{1,0:T(8,128)(2,1)} %param.8) | copy-start | bytes 3932164
  6.5 146.1 %copy-start.2 = (f32[5120]{0:T(1024)S(1)}, f32[5120]{0:T(1024)}, u32[]{:S(2)}) copy-start(f32[5120]{0:T(1024)} %param.9) | copy-start | bytes 61444
  6.5 313.7 %all-gather.2.cloned.1.call-start = ((), (), s32[]{:S(2)}) async-start(), calls=%async_computation | async-start | bytes 10813440 | tf_op jit(solution)/shard_map/all_gather | solution.py:38
  216.2 205.2 %all-reduce.3.cloned.1.call-start = ((), (), s32[]{:S(2)}) async-start(), calls=%async_computation.1 | async-start | bytes 1310720 | tf_op jit(solution)/shard_map/psum | solution.py:40
  332.7 88.7 %copy-start.1 = (bf16[1280,128]{1,0:T(8,128)(2,1)S(1)}, bf16[1280,128]{1,0:T(8,128)(2,1)}, u32[]{:S(2)}) copy-start(bf16[1280,128]{1,0:T(8,128)(2,1)} %all-reduce.4) | copy-start | bytes 983044
Sparse Core Ops, SparseCore 0:
  216.3 103.8 all-gather.1
  344.7 76.6 all-reduce.2
where the time goes:
time: 432 us; the launch traced here: 430 us
  waiting for transfers between devices  181 us (42%)
  blocking collectives  175 us (41%)
  local copies, waits for them, and re-layouts  25.8 us (6%)
  matrix products  23.2 us (5%)
  between operations  13.5 us (3%)
  other arithmetic  12.1 us (3%)
    psum x1, blocking collectives, body(): totals = lax.psum(partial_totals, 'row')  134 us
    all_gather x1, waiting for transfers between devices, body(): gathered = lax.all_gather(layer_one, 'row', axis=0, tiled=True)  104 us
    psum x1, waiting for transfers between devices, body(): layer_two = lax.psum(local_layer(needed), 'col')  76.8 us
    psum x1, blocking collectives, body(): layer_one = lax.psum(part_one, 'col').astype(jnp.bfloat16)  40.3 us
    dot_general x2, matrix products, local_layer(): jnp.einsum('bsij,bsjk->bik', coefficients, picked, preferred_element_type...  22.7 us
    gather x2, local copies, waits for them, and re-layouts, local_layer(): picked = source.reshape(group_blocks, block_size, demand_width)[slot_cols]  22.2 us
  transfers between devices with their start and end apart: 2, of which 2 were waited for; matrix products, arithmetic and copies ran while one was open for 0% of the time, Pallas kernels for 0%

commit v1 on v0

v1 whole, which is shorter than its diff:
```python
import functools

import jax
import jax.numpy as jnp
from jax import lax
from jax.experimental import pallas as pl
from jax.experimental.pallas import tpu as pltpu
from jax.sharding import PartitionSpec as P

MESH = pl.DeviceIdType.MESH
HIGH = 2
CORES = 2


def kernel(
    rows, n,
    blocks, cols_s, cols_v, counts_s, demand, added, out,
    zbuf, sums, tsend, trecv, qsend, qrecv, tall, spread, scaled,
    part, rs_recv, part2, rs_recv2, zg, source, piece,
    zsem, t_send, t_recv, q_send, q_recv, a_send, a_recv,
    rs_send, rs_sem, rs_send2, rs_sem2, g_send, g_recv, p_send, p_recv,
    c_send, c_recv, o_send, o_recv, o_local,
):
    zs = rows // (HIGH * CORES)
    rb, slots, bs = zbuf.shape[0], zbuf.shape[1], zbuf.shape[2]
    cb = demand.shape[0]
    per_z = cb // zs
    targets = n // HIGH
    span = zs // targets
    tile = bs // n
    batches = rs_sem.shape[0]
    step = rb // batches
    row, col = lax.axis_index("row"), lax.axis_index("col")
    core = row % CORES
    z = (row // CORES) % zs
    high = row // (CORES * zs)

    def rid(h, zz, k):
        return (h * zs + zz) * CORES + k

    def remote(src, dst, send, recv, to):
        return pltpu.make_async_remote_copy(
            src_ref=src, dst_ref=dst, send_sem=send, recv_sem=recv, device_id=to, device_id_type=MESH
        )

    def each(count, fn, first=0):
        def body(i, c):
            fn(i)
            return c

        lax.fori_loop(first, count, body, 0)

    def load(b):
        return pltpu.make_async_copy(blocks.at[b], zbuf.at[b], zsem.at[b])

    each(rb, lambda b: load(b).start())

    barrier = pltpu.get_barrier_semaphore()

    def greet(to):
        pl.semaphore_signal(barrier, inc=1, device_id=to, device_id_type=MESH)

    each(zs, lambda d: greet((rid(high, (z + d) % zs, core), col)), 1)
    greet((rid(high, z, 1 - core), col))
    greet((rid(1 - high, z, 1 - core), col))
    each(n, lambda d: greet((row, (col + d) % n)), 1)
    each(n, lambda d: greet((rid(1 - high, z, core), d)))

    group = lax.broadcasted_iota(jnp.int32, (cb, slots), 0)
    slot = lax.broadcasted_iota(jnp.int32, (cb, slots), 1)

    def add_row(b, total):
        load(b).wait()
        for s in range(slots):
            sums[pl.ds(s, 1), :] = jnp.sum(zbuf[b, s].astype(jnp.float32), axis=0, keepdims=True)
        hit = (group == cols_v[pl.ds(b, 1), :]) & (slot < counts_s[b, 0])
        return total + jnp.dot(
            hit.astype(jnp.float32), sums[...], precision=lax.Precision.HIGHEST,
            preferred_element_type=jnp.float32,
        )

    total = lax.fori_loop(0, rb, add_row, jnp.zeros((cb, bs), jnp.float32))
    for k in range(zs):
        tsend[k] = total[k * per_z : (k + 1) * per_z]

    pl.semaphore_wait(barrier, (zs - 1) + 2 + (n - 1) + n)

    def t_copy(d):
        to = (z + d) % zs
        return remote(
            tsend.at[to], trecv.at[d - 1], t_send.at[d - 1], t_recv.at[d - 1], (rid(high, to, core), col)
        )

    each(zs, lambda d: t_copy(d).start(), 1)
    each(zs, lambda d: t_copy(d).wait(), 1)
    mine = tsend[z]
    for d in range(zs - 1):
        mine = mine + trecv[d]
    qsend[...] = mine
    quad = [
        remote(qsend, qrecv.at[i], q_send.at[i], q_recv.at[i], (rid(h, z, k), col))
        for i, (h, k) in enumerate(((high, 1 - core), (1 - high, core), (1 - high, 1 - core)))
    ]
    for copy in quad:
        copy.start()
    for copy in quad:
        copy.wait()
    tall[z] = (mine + qrecv[0]) + (qrecv[1] + qrecv[2])

    def a_copy(d):
        return remote(
            tall.at[z], tall.at[z], a_send.at[d - 1], a_recv.at[d - 1], (rid(high, (z + d) % zs, core), col)
        )

    def a_arrived(d):
        at = tall.at[(z + zs - d) % zs]
        remote(at, at, a_send.at[d - 1], a_recv.at[d - 1], (row, col)).wait_recv()

    each(zs, lambda d: a_copy(d).start(), 1)
    each(zs, a_arrived, 1)
    each(zs, lambda d: a_copy(d).wait_send(), 1)

    totals = jnp.concatenate([tall[k] for k in range(zs)], axis=0) + added[...]
    inverse = 1.0 / totals
    padded = jnp.concatenate([inverse, jnp.zeros((bs - cb, bs), jnp.float32)], axis=0)
    turned = padded.T
    for j in range(cb):
        wide = jnp.broadcast_to(turned[:, j : j + 1], (bs, bs))
        spread[j] = wide
        scaled[j] = (demand[j].astype(jnp.float32) * wide).astype(jnp.bfloat16)
    scaled[cb] = jnp.zeros((bs, bs), jnp.bfloat16)

    def layer(into, recv, send_sem, recv_sem):
        def rs_copy(batch, d):
            to = (col + d) % n
            at = pl.ds(batch * step, step)
            return remote(
                into.at[at, to], recv.at[d - 1, at], send_sem.at[batch, d - 1], recv_sem.at[batch, d - 1],
                (row, to),
            )

        def one(b):
            live = counts_s[b, 0]
            acc = jnp.zeros((bs, bs), jnp.float32)
            for s in range(0, slots, 2):
                at = [jnp.where(t < live, cols_s[b, t], cb) for t in (s, s + 1)]
                left = jnp.concatenate([zbuf[b, s], zbuf[b, s + 1]], axis=1)
                right = jnp.concatenate([scaled[at[0]], scaled[at[1]]], axis=0)
                acc = acc + jnp.dot(left, right, preferred_element_type=jnp.float32)
            into[b] = acc.astype(jnp.bfloat16).reshape(n, tile, bs)

        for batch in range(batches):
            each((batch + 1) * step, one, batch * step)
            each(n, lambda d, batch=batch: rs_copy(batch, d).start(), 1)
        for batch in range(batches):
            each(n, lambda d, batch=batch: rs_copy(batch, d).wait(), 1)

    def summed(b, own, recv):
        acc = own[b, col].astype(jnp.float32)
        for d in range(n - 1):
            acc = acc + recv[d, b].astype(jnp.float32)
        return acc

    layer(part, rs_recv, rs_send, rs_sem)
    for b in range(rb):
        zg[z, b] = summed(b, part, rs_recv).astype(jnp.bfloat16)

    def g_copy(d):
        return remote(
            zg.at[z], zg.at[z], g_send.at[d - 1], g_recv.at[d - 1], (rid(high, (z + d) % zs, core), col)
        )

    def g_arrived(d):
        at = zg.at[(z + zs - d) % zs]
        remote(at, at, g_send.at[d - 1], g_recv.at[d - 1], (row, col)).wait_recv()

    each(zs, lambda d: g_copy(d).start(), 1)
    each(zs, g_arrived, 1)
    each(zs, lambda d: g_copy(d).wait_send(), 1)

    def p_parts(i):
        h, k = i // targets, i % targets
        to = high * targets + k
        here = (h == high) & (to == col)
        src = zg.at[pl.ds(k * span, span)]
        dst = source.at[:, core, :, col]
        far = remote(src, dst, p_send.at[i], p_recv.at[col], (rid(h, z, core), to))
        near = pltpu.make_async_copy(src, dst, p_recv.at[col])
        return here, far, near

    def p_start(i):
        here, far, near = p_parts(i)

        @pl.when(here)
        def _():
            near.start()

        @pl.when(jnp.logical_not(here))
        def _():
            far.start()

    each(n, p_start)

    def c_copy(c):
        at = source.at[:, core, :, c]
        return remote(at, at, c_send.at[c], c_recv.at[c], (rid(high, z, 1 - core), col))

    def forward(c):
        at = source.at[:, core, :, c]
        pltpu.make_async_copy(at, at, p_recv.at[c]).wait()
        c_copy(c).start()

    each(n, forward)

    def c_arrived(c):
        at = source.at[:, 1 - core, :, c]
        remote(at, at, c_send.at[c], c_recv.at[c], (row, col)).wait_recv()

    each(n, c_arrived)

    def p_sent(i):
        here, far, near = p_parts(i)

        @pl.when(jnp.logical_not(here))
        def _():
            far.wait_send()

    each(n, p_sent)
    each(n, lambda c: c_copy(c).wait_send())

    def scale(j):
        q, b = j // rb, j % rb
        value = source[q // CORES, q % CORES, b].reshape(bs, bs).astype(jnp.float32)
        scaled[j] = (value * spread[j]).astype(jnp.bfloat16)

    each(cb, scale)

    layer(part2, rs_recv2, rs_send2, rs_sem2)
    for b in range(rb):
        piece[b] = (zg[z, b].astype(jnp.float32) + summed(b, part2, rs_recv2)).astype(jnp.bfloat16)

    def o_copy(d):
        return remote(
            piece, out.at[:, col], o_send.at[d - 1], o_recv.at[d - 1], (row, (col + d) % n)
        )

    def o_arrived(d):
        at = out.at[:, (col + n - d) % n]
        remote(piece, at, o_send.at[d - 1], o_recv.at[d - 1], (row, col)).wait_recv()

    each(n, lambda d: o_copy(d).start(), 1)
    own = pltpu.make_async_copy(piece, out.at[:, col], o_local)
    own.start()
    each(n, o_arrived, 1)
    each(n, lambda d: o_copy(d).wait_send(), 1)
    own.wait()


def body(rows, n, blocks, slot_cols, counts, demand, value_added):
    rb, slots, bs = blocks.shape[0], blocks.shape[1], blocks.shape[2]
    cb = demand.shape[0] // bs
    zs = rows // (HIGH * CORES)
    span = zs // (n // HIGH)
    tile = bs // n
    batches = 2
    bf, f32, dma = jnp.bfloat16, jnp.float32, pltpu.SemaphoreType.DMA
    vmem, smem, hbm = (
        pl.BlockSpec(memory_space=pltpu.VMEM), pl.BlockSpec(memory_space=pltpu.SMEM), pl.BlockSpec(memory_space=pl.ANY)
    )
    result = pl.pallas_call(
        functools.partial(kernel, rows, n),
        out_shape=jax.ShapeDtypeStruct((rb, n, tile, bs), bf),
        in_specs=[hbm, smem, vmem, smem, vmem, vmem],
        out_specs=hbm,
        scratch_shapes=[
            pltpu.VMEM((rb, slots, bs, bs), bf),
            pltpu.VMEM((slots, bs), f32),
            pltpu.VMEM((zs, cb // zs, bs), f32),
            pltpu.VMEM((zs - 1, cb // zs, bs), f32),
            pltpu.VMEM((cb // zs, bs), f32),
            pltpu.VMEM((3, cb // zs, bs), f32),
            pltpu.VMEM((zs, cb // zs, bs), f32),
            pltpu.VMEM((cb, bs, bs), f32),
            pltpu.VMEM((cb + 1, bs, bs), bf),
            pltpu.VMEM((rb, n, tile, bs), bf),
            pltpu.VMEM((n - 1, rb, tile, bs), bf),
            pltpu.VMEM((rb, n, tile, bs), bf),
            pltpu.VMEM((n - 1, rb, tile, bs), bf),
            pltpu.VMEM((zs, rb, tile, bs), bf),
            pltpu.VMEM((span, CORES, rb, n, tile, bs), bf),
            pltpu.VMEM((rb, tile, bs), bf),
            dma((rb,)),
            dma((zs - 1,)), dma((zs - 1,)),
            dma((3,)), dma((3,)),
            dma((zs - 1,)), dma((zs - 1,)),
            dma((batches, n - 1)), dma((batches, n - 1)),
            dma((batches, n - 1)), dma((batches, n - 1)),
            dma((zs - 1,)), dma((zs - 1,)),
            dma((n,)), dma((n,)),
            dma((n,)), dma((n,)),
            dma((n - 1,)), dma((n - 1,)),
            dma(()),
        ],
        compiler_params=pltpu.CompilerParams(
            collective_id=0, has_side_effects=True, vmem_limit_bytes=56 * 2**20
        ),
    )(
        blocks, slot_cols, slot_cols, counts, demand.reshape(cb, bs, bs), value_added.reshape(cb, bs)
    )
    return result.reshape(rb * bs, bs)


def solution(mesh):
    rows, n = mesh.shape["row"], mesh.shape["col"]
    return jax.shard_map(
        functools.partial(body, rows, n),
        mesh=mesh,
        in_specs=(
            P("row", "col", None, None),
            P("row", "col"),
            P("row", "col"),
            P("col", None),
            P("col"),
        ),
        out_specs=P("row", None),
        check_vma=False,
    )
```

time: 432 us -> 82.4 us (0.19)
  waiting for transfers between devices: 181 us -> 0 us
  blocking collectives: 175 us -> 0 us
  Pallas kernels: 0 us -> 78.6 us
  matrix products: 23.2 us -> 0 us
  local copies, waits for them, and re-layouts: 25.8 us -> 3.05 us
  between operations: 13.5 us -> 0.01 us
  other arithmetic: 12.1 us -> 0 us
    psum x2 -> x0, blocking collectives: 175 us -> none  [the longest x1 134 us: body(): totals = lax.psum(partial_totals, 'row')]
    all_gather x1 -> x0, waiting for transfers between devices: 104 us -> none  [body(): gathered = lax.all_gather(layer_one, 'row', axis=0, tiled=True)]
    pallas_call x0 -> x1, Pallas kernels: none -> 78.6 us  [body(): pl.pallas_call(functools.partial(kernel, rows, n), out_shape=jax.ShapeDty...]
    psum x1 -> x0, waiting for transfers between devices: 76.8 us -> none  [body(): layer_two = lax.psum(local_layer(needed), 'col')]
    gather x4 -> x0, local copies, waits for them, and re-layouts: 23.3 us -> none  [the longest x2 22.2 us: local_layer(): picked = source.reshape(group_blocks, block_size, demand_width)[slot_cols]]
    dot_general x3 -> x0, matrix products: 23.2 us -> none  [the longest x2 22.7 us: local_layer(): jnp.einsum('bsij,bsjk->bik', coefficients, picked, preferred_element_type...]
    reduce_sum x1 -> x0, other arithmetic: 8.63 us -> none  [body(): jnp.sum(blocks, axis=2, dtype=jnp.float32) * live_slots[:, :, None]]
  transfers between devices with their start and end apart: 2 -> 0, of which waited for: 2 -> 0; matrix products, arithmetic and copies ran while one was open for 0% -> 0% of each run, Pallas kernels for 0% -> 0%
where the time goes in v1:
time: 82.4 us; the launch traced here: 81.6 us
  Pallas kernels  78.6 us (95%)
  local copies, waits for them, and re-layouts  3.05 us (4%)
    pallas_call x1, Pallas kernels, body(): pl.pallas_call(functools.partial(kernel, rows, n), out_shape=jax.ShapeDty...  78.6 us
    unnamed x2, local copies, waits for them, and re-layouts  3.05 us

profile of v1, /device:TPU:24, one launch (start us, length us, event | category | flops | bytes accessed | tf_op | source)
XLA Modules:
  0.0 81.6 jit_solution(10155366931331218508)
XLA Ops:
  0.0 1.3 %copy.6.counts_s = s32[10,1]{1,0:T(8,128)} copy(s32[10,1]{0,1:T(1,128)} %param.7) | data formatting | bytes 80 | tf_op args[2]
  1.3 78.6 %shard_map.55 = bf16[10,8,16,128]{3,2,1,0:T(8,128)(2,1)} custom-call(bf16[10,36,128,128]{3,2,1,0:T(8,128)(2,1)} %blocks.1, s32[10,36]{1,0:T(8,128)} %cols_v.1, s32[10,36]{1,0:T(8,128)} %cols_v.1, s32[10,1]{1,0:T(8,128)} %copy.6.counts_s, bf16[40,128,128]{2,1,0:T(8,128)(2,1)} %bitcast.4, f32[40,128]{1,0:T(8,128)} %bitcast.5), custom_call_target="tpu_custom_call" | custom-call | tf_op jit(solution)/shard_map/pallas_call | solution.py:270
  79.9 1.7 %copy.8 = bf16[1280,128]{1,0:T(8,128)(2,1)} copy(bf16[1280,128]{1,0:T(8,128)(2,1)} %bitcast.3) | data formatting | bytes 655360

commit v2 on v0

v2 whole, which is shorter than its diff:
```python
import functools

import jax
import jax.numpy as jnp
from jax import lax
from jax.experimental import pallas as pl
from jax.experimental.pallas import tpu as pltpu
from jax.sharding import PartitionSpec as P

MESH = pl.DeviceIdType.MESH
HIGH = 2
CORES = 2
WIDE = 4


def kernel(
    rows, n,
    blocks, cols_s, cols_v, counts_s, demand_hbm, added, out,
    zbuf, demand, sums, tsend, trecv, bsend, brecv, tall, spread, scaled,
    part, rs_recv, part2, rs_recv2, first, source, piece,
    zsem, dsem, t_send, t_recv, b_send, b_recv, a_send, a_recv,
    rs_send, rs_sem, rs_send2, rs_sem2, p_send, p_recv,
    y_send, y_recv, c_send, c_recv, o_send, o_recv, o_local,
):
    zs = rows // (HIGH * CORES)
    rb, slots, bs = zbuf.shape[0], zbuf.shape[1], zbuf.shape[2]
    cb = demand.shape[0]
    per_core = cb // CORES
    chips = rows // CORES
    targets = n // HIGH
    tile = bs // n
    batches = rs_sem.shape[0]
    step = rb // batches
    lag = min(2, batches - 1)
    row, col = lax.axis_index("row"), lax.axis_index("col")
    core = row % CORES
    z = (row // CORES) % zs
    high = row // (CORES * zs)

    def rid(h, zz, k):
        return (h * zs + zz) * CORES + k

    def remote(src, dst, send, recv, to):
        return pltpu.make_async_remote_copy(
            src_ref=src, dst_ref=dst, send_sem=send, recv_sem=recv, device_id=to, device_id_type=MESH
        )

    def each(count, fn, first=0):
        def body(i, c):
            fn(i)
            return c

        lax.fori_loop(first, count, body, 0)

    def load(b):
        return pltpu.make_async_copy(blocks.at[b], zbuf.at[b], zsem.at[b])

    each(rb, lambda b: load(b).start())
    load_demand = pltpu.make_async_copy(demand_hbm, demand, dsem)
    load_demand.start()

    buyer = row // (rows // n)
    side = z % HIGH
    giver = rid(col // targets, (col % targets) * HIGH + high, core)
    is_self = (side == high) & (buyer == col)
    here = row // CORES

    def chip(d):
        return ((here + d) % chips) * CORES + core

    barrier = pltpu.get_barrier_semaphore()

    def greet(to):
        pl.semaphore_signal(barrier, inc=1, device_id=to, device_id_type=MESH)

    each(chips, lambda d: greet((chip(d), col)), 1)
    greet((rid(high, z, 1 - core), col))
    each(n, lambda d: greet((row, (col + d) % n)), 1)

    def greet_giver(c):
        @pl.when(jnp.logical_not((giver == row) & (c == col)))
        def _():
            greet((giver, c))

    each(n, greet_giver)

    group = lax.broadcasted_iota(jnp.int32, (cb, slots), 0)
    slot = lax.broadcasted_iota(jnp.int32, (cb, slots), 1)

    def add_row(b, total):
        load(b).wait()
        for s in range(slots):
            sums[pl.ds(s, 1), :] = jnp.sum(zbuf[b, s].astype(jnp.float32), axis=0, keepdims=True)
        hit = (group == cols_v[pl.ds(b, 1), :]) & (slot < counts_s[0, b])
        return total + jnp.dot(
            hit.astype(jnp.float32), sums[...], precision=lax.Precision.HIGHEST,
            preferred_element_type=jnp.float32,
        )

    total = lax.fori_loop(0, rb, add_row, jnp.zeros((cb, bs), jnp.float32))
    for k in range(CORES):
        tsend[k] = total[k * per_core : (k + 1) * per_core]
    load_demand.wait()

    pl.semaphore_wait(barrier, (chips - 1) + 1 + (n - 1) + zs - jnp.where(is_self, 1, 0))

    twin = (rid(high, z, 1 - core), col)
    swap = remote(tsend.at[1 - core], trecv, t_send, t_recv, twin)
    swap.start()
    swap.wait()
    mine = tsend[core] + trecv[...]
    bsend[...] = jnp.concatenate(
        [mine, jnp.zeros((bsend.shape[0] - per_core, bs), jnp.float32)], axis=0
    ).astype(jnp.bfloat16)

    def b_copy(d):
        return remote(bsend, brecv.at[d - 1], b_send.at[d - 1], b_recv.at[d - 1], (chip(d), col))

    each(chips, lambda d: b_copy(d).start(), 1)
    each(chips, lambda d: b_copy(d).wait_recv(), 1)
    for d in range(chips - 1):
        mine = mine + brecv[d].astype(jnp.float32)[:per_core]
    tall[core] = mine
    give_half = remote(tall.at[core], tall.at[core], a_send, a_recv, twin)
    give_half.start()
    each(chips, lambda d: b_copy(d).wait_send(), 1)
    give_half.wait_send()
    remote(tall.at[1 - core], tall.at[1 - core], a_send, a_recv, twin).wait_recv()

    totals = jnp.concatenate([tall[k] for k in range(CORES)], axis=0) + added[...]
    inverse = 1.0 / totals
    padded = jnp.concatenate([inverse, jnp.zeros((bs - cb, bs), jnp.float32)], axis=0)
    turned = padded.T
    for j in range(cb):
        wide = jnp.broadcast_to(turned[:, j : j + 1], (bs, bs))
        spread[j] = wide
        scaled[j] = (demand[j].astype(jnp.float32) * wide).astype(jnp.bfloat16)
    scaled[cb] = jnp.zeros((bs, bs), jnp.bfloat16)

    def layer(into, recv, send_sem, recv_sem, finish, after):
        def rs_copy(i, d):
            to = (col + d) % n
            at = pl.ds(i * step, step)
            return remote(
                into.at[to, at], recv.at[d - 1, at], send_sem.at[i, d - 1], recv_sem.at[i, d - 1], (row, to)
            )

        def compute(i):
            accs = [jnp.zeros((bs, bs), jnp.float32) for _ in range(step)]
            wide = WIDE if slots % WIDE == 0 else 2
            for s in range(0, slots, wide):
                for k in range(step):
                    b = i * step + k
                    live = counts_s[0, b]
                    at = [jnp.where(t < live, cols_s[b, t], cb) for t in range(s, s + wide)]
                    left = jnp.concatenate([zbuf[b, t] for t in range(s, s + wide)], axis=1)
                    right = jnp.concatenate([scaled[a] for a in at], axis=0)
                    accs[k] = accs[k] + jnp.dot(left, right, preferred_element_type=jnp.float32)
            for k in range(step):
                into[:, i * step + k] = accs[k].astype(jnp.bfloat16).reshape(n, tile, bs)

        def reduce(i):
            each(n, lambda d: rs_copy(i, d).wait_recv(), 1)
            for k in range(step):
                b = i * step + k
                acc = into[col, b].astype(jnp.float32)
                for d in range(n - 1):
                    acc = acc + recv[d, b].astype(jnp.float32)
                finish(b, acc)
            after(i)

        def batch(i):
            compute(i)
            each(n, lambda d: rs_copy(i, d).start(), 1)

            @pl.when(i >= lag)
            def _():
                reduce(i - lag)

        each(batches, batch)
        each(batches, reduce, batches - lag)
        return lambda: each(batches, lambda i: each(n, lambda d: rs_copy(i, d).wait_send(), 1))

    def keep(b, acc):
        first[b] = acc.astype(jnp.bfloat16)

    def p_copy(i, d):
        src = first.at[pl.ds(i * step, step)]
        dst = source.at[side, core, i, col]
        to = (rid(side, (z + d) % zs, core), buyer)
        return src, dst, remote(src, dst, p_send.at[i, d], p_recv.at[i, col], to)

    def spread_out(i):
        src, dst, far = p_copy(i, 0)

        @pl.when(is_self)
        def _():
            pltpu.make_async_copy(src, dst, p_recv.at[i, col]).start()

        @pl.when(jnp.logical_not(is_self))
        def _():
            far.start()

        each(zs, lambda d: p_copy(i, d)[2].start(), 1)

    def spread_sent(i):
        @pl.when(jnp.logical_not(is_self))
        def _():
            p_copy(i, 0)[2].wait_send()

        each(zs, lambda d: p_copy(i, d)[2].wait_send(), 1)

    sent_one = layer(part, rs_recv, rs_send, rs_sem, keep, spread_out)

    def y_copy(i):
        at = source.at[high, core, i]
        return remote(at, at, y_send.at[i], y_recv.at[i], (rid(1 - high, z, core), col))

    def y_arrived(i):
        at = source.at[1 - high, core, i]
        remote(at, at, y_send.at[i], y_recv.at[i], (row, col)).wait_recv()

    def c_copy(i, h):
        at = source.at[h, core, i]
        return remote(at, at, c_send.at[i, h], c_recv.at[i, h], twin)

    def c_arrived(i, h):
        at = source.at[h, 1 - core, i]
        remote(at, at, c_send.at[i, h], c_recv.at[i, h], twin).wait_recv()

    def pass_on(i):
        def p_arrived(c):
            at = source.at[high, core, i, c]
            pltpu.make_async_copy(at, at, p_recv.at[i, c]).wait()

        each(n, p_arrived)
        y_copy(i).start()
        c_copy(i, high).start()

    def pass_back(i):
        y_arrived(i)
        c_copy(i, 1 - high).start()

    def both(i):
        pass_on(i)

        @pl.when(i >= 1)
        def _():
            pass_back(i - 1)

    each(batches, both)
    pass_back(batches - 1)

    def arrived(i):
        for h in range(HIGH):
            c_arrived(i, h)

    each(batches, arrived)

    def scale(j):
        q, b = j // rb, j % rb
        value = source[q // CORES, q % CORES, b // step, :, b % step]
        value = value.reshape(bs, bs).astype(jnp.float32)
        scaled[j] = (value * spread[j]).astype(jnp.bfloat16)

    each(cb, scale)

    def result(b, acc):
        piece[b] = (first[b].astype(jnp.float32) + acc).astype(jnp.bfloat16)

    def o_copy(i, d):
        at = pl.ds(i * step, step)
        return remote(
            piece.at[at], out.at[at, col], o_send.at[i, d - 1], o_recv.at[i, d - 1], (row, (col + d) % n)
        )

    def o_own(i):
        at = pl.ds(i * step, step)
        return pltpu.make_async_copy(piece.at[at], out.at[at, col], o_local.at[i])

    def give(i):
        each(n, lambda d: o_copy(i, d).start(), 1)
        o_own(i).start()

    def o_arrived(i, d):
        at = pl.ds(i * step, step)
        remote(
            piece.at[at], out.at[at, (col + n - d) % n], o_send.at[i, d - 1], o_recv.at[i, d - 1], (row, col)
        ).wait_recv()

    sent_two = layer(part2, rs_recv2, rs_send2, rs_sem2, result, give)
    each(batches, spread_sent)

    def passed(i):
        y_copy(i).wait_send()
        for h in range(HIGH):
            c_copy(i, h).wait_send()

    each(batches, passed)
    sent_one()
    sent_two()
    each(batches, lambda i: each(n, lambda d: o_arrived(i, d), 1))
    each(batches, lambda i: each(n, lambda d: o_copy(i, d).wait_send(), 1))
    each(batches, lambda i: o_own(i).wait())


def body(rows, n, blocks, slot_cols, counts, demand, value_added):
    rb, slots, bs = blocks.shape[0], blocks.shape[1], blocks.shape[2]
    cb = demand.shape[0] // bs
    zs = rows // (HIGH * CORES)
    tile = bs // n
    step = 2
    batches = rb // step
    per_core, chips = cb // CORES, rows // CORES
    bf, f32, dma = jnp.bfloat16, jnp.float32, pltpu.SemaphoreType.DMA
    vmem, smem, hbm = (
        pl.BlockSpec(memory_space=pltpu.VMEM), pl.BlockSpec(memory_space=pltpu.SMEM), pl.BlockSpec(memory_space=pl.ANY)
    )
    result = pl.pallas_call(
        functools.partial(kernel, rows, n),
        out_shape=jax.ShapeDtypeStruct((rb, n, tile, bs), bf),
        in_specs=[hbm, smem, vmem, smem, hbm, vmem],
        out_specs=hbm,
        scratch_shapes=[
            pltpu.VMEM((rb, slots, bs, bs), bf),
            pltpu.VMEM((cb, bs, bs), bf),
            pltpu.VMEM((slots, bs), f32),
            pltpu.VMEM((CORES, per_core, bs), f32),
            pltpu.VMEM((per_core, bs), f32),
            pltpu.VMEM((-(-per_core // 16) * 16, bs), bf),
            pltpu.VMEM((chips - 1, -(-per_core // 16) * 16, bs), bf),
            pltpu.VMEM((CORES, per_core, bs), f32),
            pltpu.VMEM((cb, bs, bs), f32),
            pltpu.VMEM((cb + 1, bs, bs), bf),
            pltpu.VMEM((n, rb, tile, bs), bf),
            pltpu.VMEM((n - 1, rb, tile, bs), bf),
            pltpu.VMEM((n, rb, tile, bs), bf),
            pltpu.VMEM((n - 1, rb, tile, bs), bf),
            pltpu.VMEM((rb, tile, bs), bf),
            pltpu.VMEM((HIGH, CORES, batches, n, step, tile, bs), bf),
            pltpu.VMEM((rb, tile, bs), bf),
            dma((rb,)), dma(()),
            dma(()), dma(()),
            dma((chips - 1,)), dma((chips - 1,)),
            dma(()), dma(()),
            dma((batches, n - 1)), dma((batches, n - 1)),
            dma((batches, n - 1)), dma((batches, n - 1)),
            dma((batches, zs)), dma((batches, n)),
            dma((batches,)), dma((batches,)),
            dma((batches, HIGH)), dma((batches, HIGH)),
            dma((batches, n - 1)), dma((batches, n - 1)),
            dma((batches,)),
        ],
        compiler_params=pltpu.CompilerParams(
            collective_id=0, has_side_effects=True, vmem_limit_bytes=56 * 2**20
        ),
    )(
        blocks, slot_cols, slot_cols, counts.T, demand.reshape(cb, bs, bs), value_added.reshape(cb, bs)
    )
    return result.reshape(rb * bs, bs)


def solution(mesh):
    rows, n = mesh.shape["row"], mesh.shape["col"]
    return jax.shard_map(
        functools.partial(body, rows, n),
        mesh=mesh,
        in_specs=(
            P("row", "col", None, None),
            P("row", "col"),
            P("row", "col"),
            P("col", None),
            P("col"),
        ),
        out_specs=P("row", None),
        check_vma=False,
    )
```

time: 432 us -> 72.2 us (0.17)
  the two profiles are of different devices: /device:TPU:24 before, /device:TPU:1 now
where the time goes in v2:
time: 72.2 us; the launch traced here: 72.1 us
  Pallas kernels  70.3 us (97%)
  local copies, waits for them, and re-layouts  1.72 us (2%)
    pallas_call x1, Pallas kernels, body(): pl.pallas_call(functools.partial(kernel, rows, n), out_shape=jax.ShapeDty...  70.3 us
    unnamed x1, local copies, waits for them, and re-layouts  1.72 us

profile of v2, /device:TPU:1, one launch (start us, length us, event | category | flops | bytes accessed | tf_op | source)
XLA Modules:
  0.0 72.1 jit_solution(7779524529623895161)
XLA Ops:
  0.0 70.3 %shard_map.55 = bf16[10,8,16,128]{3,2,1,0:T(8,128)(2,1)} custom-call(bf16[10,36,128,128]{3,2,1,0:T(8,128)(2,1)} %blocks.1, s32[10,36]{1,0:T(8,128)} %cols_v.1, s32[10,36]{1,0:T(8,128)} %cols_v.1, s32[1,10]{1,0:T(1,128)} %bitcast.7, bf16[40,128,128]{2,1,0:T(8,128)(2,1)} %bitcast.5, f32[40,128]{1,0:T(8,128)} %bitcast.6), custom_call_target="tpu_custom_call" | custom-call | tf_op jit(solution)/shard_map/pallas_call | solution.py:319
  70.3 1.7 %copy.7 = bf16[1280,128]{1,0:T(8,128)(2,1)} copy(bf16[1280,128]{1,0:T(8,128)(2,1)} %bitcast.4) | data formatting | bytes 655360

commit v3 on v2

v3 whole, which is shorter than its diff:
```python
import functools

import jax
import jax.numpy as jnp
from jax import lax
from jax.experimental import pallas as pl
from jax.experimental.pallas import tpu as pltpu
from jax.sharding import PartitionSpec as P

MESH = pl.DeviceIdType.MESH
HIGH = 2
CORES = 2
WIDE = 4


def kernel(
    rows, n, groups,
    blocks, cols_s, cols_v, counts_s, demand_hbm, added, out,
    zbuf, demand, sums, tsend, trecv, bsend, brecv, tall, spread, scaled,
    part, rs_recv, part2, rs_recv2, first, source, piece, places, place_s, so_far,
    zsem, dsem, place_sem, t_send, t_recv, b_send, b_recv, a_send, a_recv,
    rs_send, rs_sem, rs_send2, rs_sem2, p_send, p_recv,
    y_send, y_recv, c_send, c_recv, o_send, o_recv, o_local,
):
    zs = rows // (HIGH * CORES)
    rb, slots, bs = zbuf.shape[0], zbuf.shape[1], zbuf.shape[2]
    cb = demand.shape[0]
    per_core = cb // CORES
    chips = rows // CORES
    targets = n // HIGH
    tile = bs // n
    batches = len(groups)
    step = 2
    row, col = lax.axis_index("row"), lax.axis_index("col")
    core = row % CORES
    z = (row // CORES) % zs
    high = row // (CORES * zs)

    def rid(h, zz, k):
        return (h * zs + zz) * CORES + k

    def remote(src, dst, send, recv, to):
        return pltpu.make_async_remote_copy(
            src_ref=src, dst_ref=dst, send_sem=send, recv_sem=recv, device_id=to, device_id_type=MESH
        )

    def span(g):
        return pl.ds(groups[g][0], groups[g][1] - groups[g][0])

    def each(count, fn, first=0):
        def body(i, c):
            fn(i)
            return c

        lax.fori_loop(first, count, body, 0)

    def settle(ref, sem):
        pltpu.make_async_copy(ref, ref, sem).wait()

    def load(b):
        return pltpu.make_async_copy(blocks.at[b], zbuf.at[b], zsem.at[b])

    each(rb, lambda b: load(b).start())
    load_demand = pltpu.make_async_copy(demand_hbm, demand, dsem)
    load_demand.start()

    buyer = row // (rows // n)
    side = z % HIGH
    giver = rid(col // targets, (col % targets) * HIGH + high, core)
    is_self = (side == high) & (buyer == col)
    here = row // CORES

    def chip(d):
        return ((here + d) % chips) * CORES + core

    barrier = pltpu.get_barrier_semaphore()

    def greet(to):
        pl.semaphore_signal(barrier, inc=1, device_id=to, device_id_type=MESH)

    each(chips, lambda d: greet((chip(d), col)), 1)
    greet((rid(high, z, 1 - core), col))
    each(n, lambda d: greet((row, (col + d) % n)), 1)

    def greet_giver(c):
        @pl.when(jnp.logical_not((giver == row) & (c == col)))
        def _():
            greet((giver, c))

    each(n, greet_giver)

    group = lax.broadcasted_iota(jnp.int32, (cb, slots), 0)
    slot = lax.broadcasted_iota(jnp.int32, (cb, slots), 1)

    lane = lax.broadcasted_iota(jnp.int32, (cb, bs), 1)

    def add_row(b, carry):
        total, place = carry
        load(b).wait()
        for s in range(slots):
            sums[pl.ds(s, 1), :] = jnp.sum(zbuf[b, s].astype(jnp.float32), axis=0, keepdims=True)
        hit = (group == cols_v[pl.ds(b, 1), :]) & (slot < counts_s[0, b])
        found = jnp.sum(jnp.where(hit, slot + 1, 0), axis=1, keepdims=True)
        place = jnp.where(lane == b, found, place)
        total = total + jnp.dot(
            hit.astype(jnp.float32), sums[...], precision=lax.Precision.HIGHEST,
            preferred_element_type=jnp.float32,
        )
        return total, place

    total, place = lax.fori_loop(
        0, rb, add_row, (jnp.zeros((cb, bs), jnp.float32), jnp.zeros((cb, bs), jnp.int32))
    )
    places[...] = place
    move = pltpu.make_async_copy(places, place_s, place_sem)
    move.start()
    for k in range(CORES):
        tsend[k] = total[k * per_core : (k + 1) * per_core]
    load_demand.wait()
    move.wait()

    pl.semaphore_wait(barrier, (chips - 1) + 1 + (n - 1) + zs - jnp.where(is_self, 1, 0))

    twin = (rid(high, z, 1 - core), col)
    swap = remote(tsend.at[1 - core], trecv, t_send, t_recv, twin)
    swap.start()
    swap.wait()
    mine = tsend[core] + trecv[...]
    bsend[...] = jnp.concatenate(
        [mine, jnp.zeros((bsend.shape[0] - per_core, bs), jnp.float32)], axis=0
    ).astype(jnp.bfloat16)

    def b_copy(d):
        return remote(bsend, brecv.at[d - 1], b_send, b_recv, (chip(d), col))

    each(chips, lambda d: b_copy(d).start(), 1)
    settle(brecv, b_recv)
    for d in range(chips - 1):
        mine = mine + brecv[d].astype(jnp.float32)[:per_core]
    tall[core] = mine
    give_half = remote(tall.at[core], tall.at[core], a_send, a_recv, twin)
    give_half.start()
    settle(brecv, b_send)
    give_half.wait_send()
    remote(tall.at[1 - core], tall.at[1 - core], a_send, a_recv, twin).wait_recv()

    totals = jnp.concatenate([tall[k] for k in range(CORES)], axis=0) + added[...]
    inverse = 1.0 / totals
    padded = jnp.concatenate([inverse, jnp.zeros((bs - cb, bs), jnp.float32)], axis=0)
    turned = padded.T
    for j in range(cb):
        wide = jnp.broadcast_to(turned[:, j : j + 1], (bs, bs))
        spread[j] = wide
        scaled[j] = (demand[j].astype(jnp.float32) * wide).astype(jnp.bfloat16)
    scaled[cb] = jnp.zeros((bs, bs), jnp.bfloat16)

    def exchange(into, recv, send_sem, recv_sem, finish, after):
        def rs_copy(g, d):
            to = (col + d) % n
            at = span(g)
            return remote(into.at[to, at], recv.at[d - 1, at], send_sem.at[g], recv_sem.at[g], (row, to))

        def start(g):
            each(n, lambda d: rs_copy(g, d).start(), 1)

        def reduce(g):
            settle(recv.at[:, span(g)], recv_sem.at[g])
            for b in range(*groups[g]):
                acc = into[col, b].astype(jnp.float32)
                for d in range(n - 1):
                    acc = acc + recv[d, b].astype(jnp.float32)
                finish(b, acc)
            after(g)

        def sent():
            for g in range(batches):
                settle(recv.at[:, span(g)], send_sem.at[g])

        return start, reduce, sent

    def product(acc, b, pairs):
        left = jnp.concatenate([zbuf[b, t] for t, _ in pairs], axis=1)
        right = jnp.concatenate([scaled[a] for _, a in pairs], axis=0)
        return acc + jnp.dot(left, right, preferred_element_type=jnp.float32)

    def compute(i):
        accs = [jnp.zeros((bs, bs), jnp.float32) for _ in range(step)]
        wide = WIDE if slots % WIDE == 0 else 2
        for s in range(0, slots, wide):
            for k in range(step):
                b = i * step + k
                live = counts_s[0, b]
                pairs = [(t, jnp.where(t < live, cols_s[b, t], cb)) for t in range(s, s + wide)]
                accs[k] = product(accs[k], b, pairs)
        for k in range(step):
            part[:, i * step + k] = accs[k].astype(jnp.bfloat16).reshape(n, tile, bs)

    def keep(b, acc):
        first[b] = acc.astype(jnp.bfloat16)

    def p_copy(i, d):
        src = first.at[span(i)]
        dst = source.at[side, core, span(i), col]
        to = (rid(side, (z + d) % zs, core), buyer)
        return src, dst, remote(src, dst, p_send.at[i, jnp.minimum(d, 1)], p_recv.at[i], to)

    def spread_out(i):
        src, dst, far = p_copy(i, 0)

        @pl.when(is_self)
        def _():
            pltpu.make_async_copy(src, dst, p_recv.at[i]).start()

        @pl.when(jnp.logical_not(is_self))
        def _():
            far.start()

        each(zs, lambda d: p_copy(i, d)[2].start(), 1)

    def spread_sent(i):
        @pl.when(jnp.logical_not(is_self))
        def _():
            p_copy(i, 0)[2].wait_send()

        settle(source.at[high, core, span(i), pl.ds(0, zs - 1)], p_send.at[i, 1])

    start_one, reduce_one, sent_one = exchange(part, rs_recv, rs_send, rs_sem, keep, spread_out)
    for g in range(batches):
        each(groups[g][1] // step, compute, groups[g][0] // step)
        start_one(g)
    for g in range(batches):
        reduce_one(g)

    def y_copy(i):
        at = source.at[high, core, span(i)]
        return remote(at, at, y_send.at[i], y_recv.at[i], (rid(1 - high, z, core), col))

    def y_arrived(i):
        at = source.at[1 - high, core, span(i)]
        remote(at, at, y_send.at[i], y_recv.at[i], (row, col)).wait_recv()

    def c_copy(i, h):
        at = source.at[h, core, span(i)]
        return remote(at, at, c_send.at[i, h], c_recv.at[i, h], twin)

    def c_arrived(i, h):
        at = source.at[h, 1 - core, span(i)]
        remote(at, at, c_send.at[i, h], c_recv.at[i, h], twin).wait_recv()

    def pass_on(i):
        settle(source.at[high, core, span(i)], p_recv.at[i])
        y_copy(i).start()
        c_copy(i, high).start()

    def pass_back(i):
        y_arrived(i)
        c_copy(i, 1 - high).start()

    def result(b, acc):
        piece[b] = (first[b].astype(jnp.float32) + acc).astype(jnp.bfloat16)

    def o_copy(i, d):
        at = span(i)
        return remote(
            piece.at[at], out.at[at, col], o_send.at[i], o_recv.at[i], (row, (col + d) % n)
        )

    def o_own(i):
        at = span(i)
        return pltpu.make_async_copy(piece.at[at], out.at[at, col], o_local.at[i])

    def give(i):
        each(n, lambda d: o_copy(i, d).start(), 1)
        o_own(i).start()

    start_two, reduce_two, sent_two = exchange(part2, rs_recv2, rs_send2, rs_sem2, result, give)

    def advance(g):
        lo, hi = groups[g]
        for h in range(HIGH):
            c_arrived(g, h)
        cols_of = [q * rb + b for q in range(HIGH * CORES) for b in range(lo, hi)]
        for j in cols_of:
            q, b = j // rb, j % rb
            value = source[q // CORES, q % CORES, b].reshape(bs, bs).astype(jnp.float32)
            scaled[j] = (value * spread[j]).astype(jnp.bfloat16)

        def rows_of(i):
            accs = [so_far[i * step + k] if g else jnp.zeros((bs, bs), jnp.float32) for k in range(step)]
            for s in range(0, len(cols_of), WIDE):
                for k in range(step):
                    b = i * step + k
                    pairs = []
                    for j in cols_of[s : s + WIDE]:
                        at = place_s[j, b]
                        pairs.append((jnp.maximum(at - 1, 0), jnp.where(at > 0, j, cb)))
                    accs[k] = product(accs[k], b, pairs)
            for k in range(step):
                if g < batches - 1:
                    so_far[i * step + k] = accs[k]
                else:
                    part2[:, i * step + k] = accs[k].astype(jnp.bfloat16).reshape(n, tile, bs)

        if g < batches - 1:
            each(rb // step, rows_of)
        else:
            for k in range(batches):
                each(groups[k][1] // step, rows_of, groups[k][0] // step)
                start_two(k)

    for g in range(batches):
        pass_on(g)
        if g >= 1:
            pass_back(g - 1)
        if g >= 2:
            advance(g - 2)
    pass_back(batches - 1)
    for g in range(max(batches - 2, 0), batches):
        advance(g)
    for g in range(batches):
        reduce_two(g)

    for g in range(batches):
        spread_sent(g)

    def passed(i):
        y_copy(i).wait_send()
        for h in range(HIGH):
            c_copy(i, h).wait_send()

    for g in range(batches):
        passed(g)
    sent_one()
    sent_two()

    for g in range(batches):
        like = rs_recv2.at[:, span(g)]
        settle(like, o_recv.at[g])
        settle(like, o_send.at[g])
        o_own(g).wait()


def body(rows, n, blocks, slot_cols, counts, demand, value_added):
    rb, slots, bs = blocks.shape[0], blocks.shape[1], blocks.shape[2]
    cb = demand.shape[0] // bs
    zs = rows // (HIGH * CORES)
    tile = bs // n
    cuts = sorted({0, rb * 2 // 5 // 2 * 2, rb * 4 // 5 // 2 * 2, rb})
    groups = tuple(zip(cuts, cuts[1:]))
    batches = len(groups)
    per_core, chips = cb // CORES, rows // CORES
    bf, f32, dma = jnp.bfloat16, jnp.float32, pltpu.SemaphoreType.DMA
    vmem, smem, hbm = (
        pl.BlockSpec(memory_space=pltpu.VMEM), pl.BlockSpec(memory_space=pltpu.SMEM), pl.BlockSpec(memory_space=pl.ANY)
    )
    result = pl.pallas_call(
        functools.partial(kernel, rows, n, groups),
        out_shape=jax.ShapeDtypeStruct((rb, n, tile, bs), bf),
        in_specs=[hbm, smem, vmem, smem, hbm, vmem],
        out_specs=hbm,
        scratch_shapes=[
            pltpu.VMEM((rb, slots, bs, bs), bf),
            pltpu.VMEM((cb, bs, bs), bf),
            pltpu.VMEM((slots, bs), f32),
            pltpu.VMEM((CORES, per_core, bs), f32),
            pltpu.VMEM((per_core, bs), f32),
            pltpu.VMEM((-(-per_core // 16) * 16, bs), bf),
            pltpu.VMEM((chips - 1, -(-per_core // 16) * 16, bs), bf),
            pltpu.VMEM((CORES, per_core, bs), f32),
            pltpu.VMEM((cb, bs, bs), f32),
            pltpu.VMEM((cb + 1, bs, bs), bf),
            pltpu.VMEM((n, rb, tile, bs), bf),
            pltpu.VMEM((n - 1, rb, tile, bs), bf),
            pltpu.VMEM((n, rb, tile, bs), bf),
            pltpu.VMEM((n - 1, rb, tile, bs), bf),
            pltpu.VMEM((rb, tile, bs), bf),
            pltpu.VMEM((HIGH, CORES, rb, n, tile, bs), bf),
            pltpu.VMEM((rb, tile, bs), bf),
            pltpu.VMEM((cb, bs), jnp.int32),
            pltpu.SMEM((cb, bs), jnp.int32),
            pltpu.VMEM((rb, bs, bs), f32),
            dma((rb,)), dma(()), dma(()),
            dma(()), dma(()),
            dma(()), dma(()),
            dma(()), dma(()),
            dma((batches,)), dma((batches,)),
            dma((batches,)), dma((batches,)),
            dma((batches, 2)), dma((batches,)),
            dma((batches,)), dma((batches,)),
            dma((batches, HIGH)), dma((batches, HIGH)),
            dma((batches,)), dma((batches,)),
            dma((batches,)),
        ],
        compiler_params=pltpu.CompilerParams(
            collective_id=0, has_side_effects=True, vmem_limit_bytes=56 * 2**20
        ),
    )(
        blocks, slot_cols, slot_cols, counts.T, demand.reshape(cb, bs, bs), value_added.reshape(cb, bs)
    )
    return result.reshape(rb * bs, bs)


def solution(mesh):
    rows, n = mesh.shape["row"], mesh.shape["col"]
    return jax.shard_map(
        functools.partial(body, rows, n),
        mesh=mesh,
        in_specs=(
            P("row", "col", None, None),
            P("row", "col"),
            P("row", "col"),
            P("col", None),
            P("col"),
        ),
        out_specs=P("row", None),
        check_vma=False,
    )
```

time: 72.2 us -> 64 us (0.89)
  the two profiles are of different devices: /device:TPU:1 before, /device:TPU:24 now
where the time goes in v3:
time: 64 us; the launch traced here: 63.9 us
  Pallas kernels  62.1 us (97%)
  local copies, waits for them, and re-layouts  1.72 us (3%)
    pallas_call x1, Pallas kernels, body(): pl.pallas_call(functools.partial(kernel, rows, n, groups), out_shape=jax....  62.1 us
    unnamed x1, local copies, waits for them, and re-layouts  1.72 us

profile of v3, /device:TPU:24, one launch (start us, length us, event | category | flops | bytes accessed | tf_op | source)
XLA Modules:
  0.0 63.9 jit_solution(7102895188493440656)
XLA Ops:
  0.0 62.1 %shard_map.55 = bf16[10,8,16,128]{3,2,1,0:T(8,128)(2,1)} custom-call(bf16[10,36,128,128]{3,2,1,0:T(8,128)(2,1)} %blocks.1, s32[10,36]{1,0:T(8,128)} %cols_v.1, s32[10,36]{1,0:T(8,128)} %cols_v.1, s32[1,10]{1,0:T(1,128)} %bitcast.7, bf16[40,128,128]{2,1,0:T(8,128)(2,1)} %bitcast.5, f32[40,128]{1,0:T(8,128)} %bitcast.6), custom_call_target="tpu_custom_call" | custom-call | tf_op jit(solution)/shard_map/pallas_call | solution.py:356
  62.1 1.7 %copy.7 = bf16[1280,128]{1,0:T(8,128)(2,1)} copy(bf16[1280,128]{1,0:T(8,128)(2,1)} %bitcast.4) | data formatting | bytes 655360

commit v4 on v3

--- a/solution.py
+++ b/solution.py
@@ -39,6 +39,9 @@
     def rid(h, zz, k):
         return (h * zs + zz) * CORES + k
 
+    def wrap(i, count):
+        return jnp.where(i >= count, i - count, i)
+
     def remote(src, dst, send, recv, to):
         return pltpu.make_async_remote_copy(
             src_ref=src, dst_ref=dst, send_sem=send, recv_sem=recv, device_id=to, device_id_type=MESH
@@ -71,7 +74,7 @@
     here = row // CORES
 
     def chip(d):
-        return ((here + d) % chips) * CORES + core
+        return wrap(here + d, chips) * CORES + core
 
     barrier = pltpu.get_barrier_semaphore()
 
@@ -80,7 +83,7 @@
 
     each(chips, lambda d: greet((chip(d), col)), 1)
     greet((rid(high, z, 1 - core), col))
-    each(n, lambda d: greet((row, (col + d) % n)), 1)
+    each(n, lambda d: greet((row, wrap(col + d, n))), 1)
 
     def greet_giver(c):
         @pl.when(jnp.logical_not((giver == row) & (c == col)))
@@ -156,7 +159,7 @@
 
     def exchange(into, recv, send_sem, recv_sem, finish, after):
         def rs_copy(g, d):
-            to = (col + d) % n
+            to = wrap(col + d, n)
             at = span(g)
             return remote(into.at[to, at], recv.at[d - 1, at], send_sem.at[g], recv_sem.at[g], (row, to))
 
@@ -201,7 +204,7 @@
     def p_copy(i, d):
         src = first.at[span(i)]
         dst = source.at[side, core, span(i), col]
-        to = (rid(side, (z + d) % zs, core), buyer)
+        to = (rid(side, wrap(z + d, zs), core), buyer)
         return src, dst, remote(src, dst, p_send.at[i, jnp.minimum(d, 1)], p_recv.at[i], to)
 
     def spread_out(i):
@@ -262,7 +265,7 @@
     def o_copy(i, d):
         at = span(i)
         return remote(
-            piece.at[at], out.at[at, col], o_send.at[i], o_recv.at[i], (row, (col + d) % n)
+            piece.at[at], out.at[at, col], o_send.at[i], o_recv.at[i], (row, wrap(col + d, n))
         )
 
     def o_own(i):
@@ -310,10 +313,10 @@
 
     for g in range(batches):
         pass_on(g)
+        if g >= 2:
+            advance(g - 2)
         if g >= 1:
             pass_back(g - 1)
-        if g >= 2:
-            advance(g - 2)
     pass_back(batches - 1)
     for g in range(max(batches - 2, 0), batches):
         advance(g)

time: 64 us -> 63.6 us (level); the launches traced: 63.9 us -> 62.6 us
  Pallas kernels: 62.1 us -> 60.8 us
    pallas_call x1, Pallas kernels: 62.1 us -> 60.8 us  [body(): pl.pallas_call(functools.partial(kernel, rows, n, groups), out_shape=jax....]
where the time goes in v4:
time: 63.6 us; the launch traced here: 62.6 us
  Pallas kernels  60.8 us (96%)
  local copies, waits for them, and re-layouts  1.72 us (3%)
    pallas_call x1, Pallas kernels, body(): pl.pallas_call(functools.partial(kernel, rows, n, groups), out_shape=jax....  60.8 us
    unnamed x1, local copies, waits for them, and re-layouts  1.72 us

profile of v4, /device:TPU:24, one launch (start us, length us, event | category | flops | bytes accessed | tf_op | source)
XLA Modules:
  0.0 62.6 jit_solution(16839251858714616782)
XLA Ops:
  0.0 60.8 %shard_map.55 = bf16[10,8,16,128]{3,2,1,0:T(8,128)(2,1)} custom-call(bf16[10,36,128,128]{3,2,1,0:T(8,128)(2,1)} %blocks.1, s32[10,36]{1,0:T(8,128)} %cols_v.1, s32[10,36]{1,0:T(8,128)} %cols_v.1, s32[1,10]{1,0:T(1,128)} %bitcast.7, bf16[40,128,128]{2,1,0:T(8,128)(2,1)} %bitcast.5, f32[40,128]{1,0:T(8,128)} %bitcast.6), custom_call_target="tpu_custom_call" | custom-call | tf_op jit(solution)/shard_map/pallas_call | solution.py:359
  60.8 1.7 %copy.7 = bf16[1280,128]{1,0:T(8,128)(2,1)} copy(bf16[1280,128]{1,0:T(8,128)(2,1)} %bitcast.4) | data formatting | bytes 655360
